TPU v7x, 32 devices: a whole 2x2x4 slice. The times are simulated.
32 devices in a mesh: gx: 4 (over x, core), gy: 8 (over z, y).
Axes of the slice: x: 2, y: 2, z: 4, core: 2. Of those that a mesh axis runs over, the one named last changes fastest.
Arguments:
- nest_state: float32 [4, 8, 96, 3072], P(None, None, 'gx', 'gy'), may hold values from -6 to 6
- parent_state: float32 [4, 8, 96, 3072], P(None, None, 'gx', 'gy'), may hold values from -6 to 6
- offset_x: int32 [1], replicated, may hold values from 1 to 15
- offset_y: int32 [1], replicated, may hold values from 385 to 511
Outputs:
- nest_out: float32 [4, 8, 96, 3072], P(None, None, 'gx', 'gy')
- parent_out: float32 [4, 8, 96, 3072], P(None, None, 'gx', 'gy')
All inputs are finite; a program needn't handle non-finite values.
Results may differ from a plain program's by a relative error of at most 0.00019.
Values sent between devices are 32-bit elements; how exact they have to be, the bound alone decides.
A program may use at most 128 MiB of HBM per device.

v0:
```python
import jax
import jax.numpy as jnp
from jax import lax
from jax.sharding import PartitionSpec as P

SUBSTEPS = 3
CARRY_RATE = 0.35
SOUND_RATE = 0.4
MIXING_RATE = 0.2


def extended(value, sides, width):
    for axis, dim in sides:
        size, length = (lax.axis_size(axis), value.shape[dim])
        up = [(i, (i + 1) % size) for i in range(size - 1)]
        down = [(j, i) for i, j in up]
        last = lax.slice_in_dim(value, length - width, length, axis=dim)
        initial = lax.slice_in_dim(value, 0, width, axis=dim)
        before = lax.ppermute(last, axis, up)
        after = lax.ppermute(initial, axis, down)
        value = jnp.concatenate([before, value, after], axis=dim)
    return value


def advance(padded):
    center = padded[:, :, 1:-1, 1:-1]
    slope_x = (padded[:, :, 2:, 1:-1] - padded[:, :, :-2, 1:-1]) * 0.5
    slope_y = (padded[:, :, 1:-1, 2:] - padded[:, :, 1:-1, :-2]) * 0.5
    carried = center[0][None] * slope_x[:3] + center[1][None] * slope_y[:3]
    potential = center[2]
    level_above = jnp.concatenate([potential[1:], potential[-1:]], axis=0)
    level_below = jnp.concatenate([potential[:1], potential[:-1]], axis=0)
    wind_east = center[0] - CARRY_RATE * carried[0] - SOUND_RATE * slope_x[3]
    wind_north = center[1] - CARRY_RATE * carried[1] - SOUND_RATE * slope_y[3]
    heat_next = (
        potential
        - CARRY_RATE * carried[2]
        + MIXING_RATE * (level_above - 2.0 * potential + level_below)
    )
    pressure = center[3] - SOUND_RATE * (slope_x[0] + slope_y[1])
    return jnp.stack([wind_east, wind_north, heat_next, pressure])


def place_along(piece, first, width, axis):
    length = piece.shape[axis]
    target = lax.broadcasted_iota(jnp.int32, (length, width), 0) - first
    places = lax.broadcasted_iota(jnp.int32, (length, width), 1)
    table = (target == places).astype(jnp.float32)
    moved = jnp.moveaxis(piece, axis, -1)
    placed = jnp.dot(
        moved, table, precision=lax.Precision.HIGHEST, preferred_element_type=jnp.float32
    )
    return jnp.moveaxis(placed, -1, axis)


def on_device(nest_state, parent_state, offset_x, offset_y):
    shift_x = offset_x[0]
    shift_y = offset_y[0]
    count_x = lax.axis_size("gx")
    count_y = lax.axis_size("gy")
    index_x = lax.axis_index("gx")
    index_y = lax.axis_index("gy")
    levels = nest_state.shape[1]
    nest_cols = nest_state.shape[2]
    nest_rows = nest_state.shape[3]
    parent_cols = parent_state.shape[2]
    parent_rows = parent_state.shape[3]
    coarse_cols = nest_cols // 3
    coarse_rows = nest_rows // 3
    span_x = count_x * coarse_cols
    span_y = count_y * coarse_rows

    def take_slab(wanted, owner_index, extent, axis):
        local = wanted - owner_index * extent
        inside = (local >= 0) & (local < extent)
        slab = lax.dynamic_slice_in_dim(parent_state, jnp.clip(local, 0, extent - 1), 1, axis)
        return jnp.where(inside, jnp.squeeze(slab, axis), 0.0)

    columns = jnp.stack(
        [
            take_slab(shift_x - 1, index_x, parent_cols, 2),
            take_slab(shift_x + span_x, index_x, parent_cols, 2),
        ]
    )
    columns = lax.psum(columns, "gx")
    row_pair = jnp.stack(
        [
            take_slab(shift_y - 1, index_y, parent_rows, 3),
            take_slab(shift_y + span_y, index_y, parent_rows, 3),
        ]
    )
    row_pair = lax.psum(row_pair, "gy")
    column_first = shift_y + index_y * coarse_rows - 1
    row_first = shift_x + index_x * coarse_cols - 1
    column_strip = place_along(
        lax.all_gather(columns, "gy", axis=3, tiled=True), column_first, coarse_rows + 2, 3
    )
    row_strip = place_along(
        lax.all_gather(row_pair, "gx", axis=3, tiled=True), row_first, coarse_cols + 2, 3
    )
    column_strip = jnp.repeat(column_strip, 3, axis=3)
    row_strip = jnp.repeat(row_strip, 3, axis=3)
    parent_padded = extended(parent_state, (("gx", 2), ("gy", 3)), 1)
    parent_next = advance(parent_padded)
    fields = nest_state
    for substep in range(SUBSTEPS):
        padded = extended(fields, (("gx", 2), ("gy", 3)), 1)
        col_pos = lax.broadcasted_iota(jnp.int32, (padded.shape[2], 1), 0)
        row_pos = lax.broadcasted_iota(jnp.int32, (1, padded.shape[3]), 1)
        lower = 3 - 1
        west = column_strip[0][:, :, None, lower : lower + nest_rows + 2 * 1]
        east = column_strip[1][:, :, None, lower : lower + nest_rows + 2 * 1]
        south = row_strip[0][:, :, lower : lower + nest_cols + 2 * 1, None]
        north = row_strip[1][:, :, lower : lower + nest_cols + 2 * 1, None]
        result = jnp.where((index_x == 0) & (col_pos < 1), west, padded)
        result = jnp.where((index_x == count_x - 1) & (col_pos >= nest_cols + 1), east, result)
        result = jnp.where((index_y == 0) & (row_pos < 1), south, result)
        result = jnp.where((index_y == count_y - 1) & (row_pos >= nest_rows + 1), north, result)
        fields = advance(result)
    coarse = fields[:3].reshape(3, levels, coarse_cols, 3, coarse_rows, 3).mean(axis=(3, 5))
    col_first = index_x * parent_cols - shift_x
    rows_first = index_y * parent_rows - shift_y
    partial_block = place_along(
        lax.all_gather(coarse, "gy", axis=3, tiled=True), rows_first, parent_rows, 3
    )
    returned = place_along(
        lax.all_gather(partial_block, "gx", axis=2, tiled=True), col_first, parent_cols, 2
    )
    col_global = index_x * parent_cols + lax.broadcasted_iota(jnp.int32, (parent_cols, 1), 0)
    row_global = index_y * parent_rows + lax.broadcasted_iota(jnp.int32, (1, parent_rows), 1)
    inside = (
        (col_global >= shift_x)
        & (col_global < shift_x + span_x)
        & (row_global >= shift_y)
        & (row_global < shift_y + span_y)
    )
    blended = jnp.where(inside, returned, parent_next[:3])
    parent_out = jnp.concatenate([blended, parent_next[3:]], axis=0)
    return (fields, parent_out)


def solution(mesh):
    placed = (P(None, None, "gx", "gy"), P(None, None, "gx", "gy"), P(), P())
    return jax.shard_map(
        on_device,
        mesh=mesh,
        in_specs=placed,
        out_specs=(P(None, None, "gx", "gy"), P(None, None, "gx", "gy")),
        check_vma=False,
    )
```

profile of v0, /device:TPU:0, one launch (start us, length us, event | category | flops | bytes accessed | tf_op | source)
XLA Modules:
  0.0 323.4 jit_solution(11506212641012016978)
XLA Ops:
  8.0 2.2 fusion.95
  12.1 2.4 collective-permute-start
  14.4 1.3 collective-permute-start.1
  17.4 39.1 %psum.14 = f32[2,4,8,24]{2,1,0,3:T(4,128)S(1)} all-reduce(f32[2,4,8,24]{2,1,0,3:T(4,128)S(1)} %copy.41), channel_id=1, replica_groups=mesh['gx'=4,'gy'=8] {'gy'}, use_global_device_ids=true, to_apply=%region_0.1 | all-reduce | flops 1536 | bytes 12288 | tf_op jit(solution)/shard_map/psum | solution.py:92
  56.5 9.2 %all_gather.12 = f32[2,4,8,96]{2,1,0,3:T(4,128)S(1)} all-gather(f32[2,4,8,24]{2,1,0,3:T(4,128)S(1)} %psum.14), channel_id=1, replica_groups=mesh['gx'=4,'gy'=8] {'gx'}, dimensions={3}, use_global_device_ids=true | all-gather | bytes 30720 | tf_op jit(solution)/shard_map/all_gather | solution.py:99
  67.9 2.1 collective-permute-start.2
  71.3 50.3 %all_gather.13 = f32[2,4,8,3072]{3,2,1,0:T(8,128)S(1)} all-gather(f32[2,4,8,384]{3,2,1,0:T(8,128)} %all-reduce.2.cloned.1.call-done), channel_id=1, replica_groups=mesh['gx'=4,'gy'=8] {'gy'}, dimensions={3}, use_global_device_ids=true | all-gather | bytes 884736 | tf_op jit(solution)/shard_map/all_gather | solution.py:96
  124.2 3.1 fusion.2
  129.6 1.3 collective-permute-start.4
  130.9 1.3 collective-permute-start.5
  132.2 1.3 collective-permute-start.12
  133.5 5.1 %collective-permute-start.13 = (f32[4,8,1,384]{3,2,1,0:T(1,128)}, f32[4,8,1,384]{3,2,1,0:T(1,128)S(1)}, u32[]{:S(2)}, u32[]{:S(2)}) collective-permute-start(f32[4,8,1,384]{3,2,1,0:T(1,128)} %get-tuple-element.58), channel_id=1, source_target_pairs={{0,8},{8,16},{16,24},{1,9},{9,17},{17,25},{2,10},{10,18},{18,26},{... | collective-permute-start | bytes 147464 | tf_op jit(solution)/shard_map/ppermute | solution.py:19
  138.9 1.3 collective-permute-start.6
  140.3 1.5 collective-permute-start.7
  142.6 20.1 %collective-permute-done.6 = f32[4,8,26,1]{3,2,1,0:T(8,128)S(1)} collective-permute-done((f32[4,8,26,1]{3,2,1,0:T(8,128)S(1)}, f32[4,8,26,1]{3,2,1,0:T(8,128)S(1)}, u32[]{:S(2)}, u32[]{:S(2)}) %collective-permute-start.6) | collective-permute-done | bytes 3360 | tf_op jit(solution)/shard_map/ppermute | solution.py:19
  162.7 2.6 fusion.5
  167.7 3.1 collective-permute-start.8
  170.8 1.3 collective-permute-start.9
  172.7 1.5 collective-permute-done.9
  174.5 4.4 %collective-permute-start.10 = (f32[4,8,26,1]{3,2,1,0:T(8,128)S(1)}, f32[4,8,26,1]{3,2,1,0:T(8,128)S(1)}, u32[]{:S(2)}, u32[]{:S(2)}) collective-permute-start(f32[4,8,26,1]{3,2,1,0:T(8,128)S(1)} %get-tuple-element.46), channel_id=1, source_target_pairs={{0,1},{1,2},{2,3},{3,4},{4,5},{5,6},{6,7},{8,9},{9,10},{10,11},{11... | collective-permute-start | bytes 9992 | tf_op jit(solution)/shard_map/ppermute | solution.py:19
  178.9 1.3 collective-permute-start.11
  180.3 20.3 %collective-permute-done.10 = f32[4,8,26,1]{3,2,1,0:T(8,128)S(1)} collective-permute-done((f32[4,8,26,1]{3,2,1,0:T(8,128)S(1)}, f32[4,8,26,1]{3,2,1,0:T(8,128)S(1)}, u32[]{:S(2)}, u32[]{:S(2)}) %collective-permute-start.10) | collective-permute-done | bytes 3360 | tf_op jit(solution)/shard_map/ppermute | solution.py:19
  200.6 2.6 fusion.8
  206.2 8.3 %copy.53 = f32[3,8,24,384]{1,3,2,0:T(8,128)} copy(f32[3,8,24,384]{3,2,1,0:T(8,128)S(1)} %pad_maximum_fusion.10) | data formatting | bytes 1769472 | tf_op jit(solution)/shard_map/stack | solution.py:41
  214.4 21.9 %reshape.170 = f32[3,8,8,3,128,3]{1,5,4,3,2,0:T(4,128)} reshape(f32[3,8,24,384]{1,3,2,0:T(8,128)} %copy.53) | data formatting | bytes 1769472 | tf_op jit(solution)/shard_map/reshape | solution.py:120
  236.3 14.8 %reduce_sum.9 = f32[3,8,8,128]{1,3,2,0:T(8,128)S(1)} reduce(f32[3,8,8,3,128,3]{1,5,4,3,2,0:T(4,128)} %reshape.170, f32[]{:T(128)} %constant.17.clone.1), dimensions={3,5}, to_apply=%region_2.3 | reduce | flops 196608 | bytes 983044 | tf_op jit(solution)/shard_map/reduce_sum | solution.py:120
  251.6 36.0 %all_gather.14 = f32[3,8,8,1024]{3,2,1,0:T(8,128)S(1)} all-gather(f32[3,8,8,128]{3,2,1,0:T(8,128)S(1)} %broadcast_multiply_fusion), channel_id=1, replica_groups=mesh['gx'=4,'gy'=8] {'gy'}, dimensions={3}, use_global_device_ids=true | all-gather | bytes 884736 | tf_op jit(solution)/shard_map/all_gather | solution.py:124
  287.6 1.7 fusion.13
  291.1 4.6 %collective-permute-start.15 = (f32[4,8,26,1]{3,2,1,0:T(8,128)S(1)}, f32[4,8,26,1]{3,2,1,0:T(8,128)S(1)}, u32[]{:S(2)}, u32[]{:S(2)}) collective-permute-start(f32[4,8,26,1]{3,2,1,0:T(8,128)S(1)} %get-tuple-element.45), channel_id=1, source_target_pairs={{0,1},{1,2},{2,3},{3,4},{4,5},{5,6},{6,7},{8,9},{9,10},{10,11},{11... | collective-permute-start | bytes 9992 | tf_op jit(solution)/shard_map/ppermute | solution.py:19
  295.7 5.2 %collective-permute-done.14 = f32[4,8,26,1]{3,2,1,0:T(8,128)S(1)} collective-permute-done((f32[4,8,26,1]{3,2,1,0:T(8,128)S(1)}, f32[4,8,26,1]{3,2,1,0:T(8,128)S(1)}, u32[]{:S(2)}, u32[]{:S(2)}) %collective-permute-start.14) | collective-permute-done | bytes 3360 | tf_op jit(solution)/shard_map/ppermute | solution.py:20
  300.9 8.2 %collective-permute-done.15 = f32[4,8,26,1]{3,2,1,0:T(8,128)S(1)} collective-permute-done((f32[4,8,26,1]{3,2,1,0:T(8,128)S(1)}, f32[4,8,26,1]{3,2,1,0:T(8,128)S(1)}, u32[]{:S(2)}, u32[]{:S(2)}) %collective-permute-start.15) | collective-permute-done | bytes 3360 | tf_op jit(solution)/shard_map/ppermute | solution.py:19
  313.6 1.8 fusion.15
  (112 shorter events, 26.2 us)
Async XLA Ops:
  7.2 9.3 %copy-start = (f32[4,8,24,384]{3,2,1,0:T(8,128)S(1)}, f32[4,8,24,384]{3,2,1,0:T(8,128)}, u32[]{:S(2)}) copy-start(f32[4,8,24,384]{3,2,1,0:T(8,128)} %param.5) | copy-start | bytes 3538948
  7.2 64.1 %all-reduce.2.cloned.1.call-start = ((), (), s32[]{:S(2)}) async-start(), calls=%async_computation | async-start | bytes 196608 | tf_op jit(solution)/shard_map/psum | solution.py:85
  10.8 302.8 %all-gather.2.cloned.1.call-start = ((), (), s32[]{:S(2)}) async-start(), calls=%async_computation.1 | async-start | bytes 1474560 | tf_op jit(solution)/shard_map/all_gather | solution.py:127
  12.1 54.6 %collective-permute-start = (f32[4,8,1,384]{3,2,1,0:T(1,128)S(1)}, f32[4,8,1,384]{3,2,1,0:T(1,128)S(1)}, u32[]{:S(2)}, u32[]{:S(2)}) collective-permute-start(f32[4,8,1,384]{3,2,1,0:T(1,128)S(1)} %get-tuple-element.68), channel_id=1, source_target_pairs={{0,8},{8,16},{16,24},{1,9},{9,17},{17,25},{2,10},{10,18},{18,26},{... | collective-permute-start | bytes 147464 | tf_op jit(solution)/shard_map/ppermute | solution.py:19
  14.4 52.2 %collective-permute-start.1 = (f32[4,8,1,384]{3,2,1,0:T(1,128)S(1)}, f32[4,8,1,384]{3,2,1,0:T(1,128)S(1)}, u32[]{:S(2)}, u32[]{:S(2)}) collective-permute-start(f32[4,8,1,384]{3,2,1,0:T(1,128)S(1)} %get-tuple-element.69), channel_id=1, source_target_pairs={{8,0},{16,8},{24,16},{9,1},{17,9},{25,17},{10,2},{18,10},{26,18},{... | collective-permute-start | bytes 147464 | tf_op jit(solution)/shard_map/ppermute | solution.py:20
  17.0 49.7 %copy-start.1 = (f32[4,8,24,384]{3,2,1,0:T(8,128)S(1)}, f32[4,8,24,384]{3,2,1,0:T(8,128)}, u32[]{:S(2)}) copy-start(f32[4,8,24,384]{3,2,1,0:T(8,128)} %param.4) | copy-start | bytes 3538948
  67.9 56.3 %collective-permute-start.2 = (f32[4,8,26,1]{3,2,1,0:T(8,128)}, f32[4,8,26,1]{3,2,1,0:T(8,128)}, u32[]{:S(2)}, u32[]{:S(2)}) collective-permute-start(f32[4,8,26,1]{3,2,1,0:T(8,128)} %get-tuple-element.50), channel_id=1, source_target_pairs={{0,1},{1,2},{2,3},{3,4},{4,5},{5,6},{6,7},{8,9},{9,10},{10,11},{11... | collective-permute-start | bytes 9992 | tf_op jit(solution)/shard_map/ppermute | solution.py:19
  70.0 54.2 %collective-permute-start.3 = (f32[4,8,26,1]{3,2,1,0:T(8,128)}, f32[4,8,26,1]{3,2,1,0:T(8,128)}, u32[]{:S(2)}, u32[]{:S(2)}) collective-permute-start(f32[4,8,26,1]{3,2,1,0:T(8,128)} %get-tuple-element.51), channel_id=1, source_target_pairs={{1,0},{2,1},{3,2},{4,3},{5,4},{6,5},{7,6},{9,8},{10,9},{11,10},{12... | collective-permute-start | bytes 9992 | tf_op jit(solution)/shard_map/ppermute | solution.py:20
  129.6 9.0 %collective-permute-start.4 = (f32[4,8,1,384]{3,2,1,0:T(1,128)S(1)}, f32[4,8,1,384]{3,2,1,0:T(1,128)S(1)}, u32[]{:S(2)}, u32[]{:S(2)}) collective-permute-start(f32[4,8,1,384]{3,2,1,0:T(1,128)S(1)} %get-tuple-element.64), channel_id=1, source_target_pairs={{0,8},{8,16},{16,24},{1,9},{9,17},{17,25},{2,10},{10,18},{18,26},{... | collective-permute-start | bytes 147464 | tf_op jit(solution)/shard_map/ppermute | solution.py:19
  130.9 7.7 %collective-permute-start.5 = (f32[4,8,1,384]{3,2,1,0:T(1,128)S(1)}, f32[4,8,1,384]{3,2,1,0:T(1,128)S(1)}, u32[]{:S(2)}, u32[]{:S(2)}) collective-permute-start(f32[4,8,1,384]{3,2,1,0:T(1,128)S(1)} %get-tuple-element.65), channel_id=1, source_target_pairs={{8,0},{16,8},{24,16},{9,1},{17,9},{25,17},{10,2},{18,10},{26,18},{... | collective-permute-start | bytes 147464 | tf_op jit(solution)/shard_map/ppermute | solution.py:20
  132.2 157.3 %collective-permute-start.12 = (f32[4,8,1,384]{3,2,1,0:T(1,128)}, f32[4,8,1,384]{3,2,1,0:T(1,128)S(1)}, u32[]{:S(2)}, u32[]{:S(2)}) collective-permute-start(f32[4,8,1,384]{3,2,1,0:T(1,128)} %get-tuple-element.59), channel_id=1, source_target_pairs={{8,0},{16,8},{24,16},{9,1},{17,9},{25,17},{10,2},{18,10},{26,18},{... | collective-permute-start | bytes 147464 | tf_op jit(solution)/shard_map/ppermute | solution.py:20
  133.5 156.0 %collective-permute-start.13 = (f32[4,8,1,384]{3,2,1,0:T(1,128)}, f32[4,8,1,384]{3,2,1,0:T(1,128)S(1)}, u32[]{:S(2)}, u32[]{:S(2)}) collective-permute-start(f32[4,8,1,384]{3,2,1,0:T(1,128)} %get-tuple-element.58), channel_id=1, source_target_pairs={{0,8},{8,16},{16,24},{1,9},{9,17},{17,25},{2,10},{10,18},{18,26},{... | collective-permute-start | bytes 147464 | tf_op jit(solution)/shard_map/ppermute | solution.py:19
  138.9 23.8 %collective-permute-start.6 = (f32[4,8,26,1]{3,2,1,0:T(8,128)S(1)}, f32[4,8,26,1]{3,2,1,0:T(8,128)S(1)}, u32[]{:S(2)}, u32[]{:S(2)}) collective-permute-start(f32[4,8,26,1]{3,2,1,0:T(8,128)S(1)} %get-tuple-element.48), channel_id=1, source_target_pairs={{0,1},{1,2},{2,3},{3,4},{4,5},{5,6},{6,7},{8,9},{9,10},{10,11},{11... | collective-permute-start | bytes 9992 | tf_op jit(solution)/shard_map/ppermute | solution.py:19
  140.3 22.5 %collective-permute-start.7 = (f32[4,8,26,1]{3,2,1,0:T(8,128)S(1)}, f32[4,8,26,1]{3,2,1,0:T(8,128)S(1)}, u32[]{:S(2)}, u32[]{:S(2)}) collective-permute-start(f32[4,8,26,1]{3,2,1,0:T(8,128)S(1)} %get-tuple-element.49), channel_id=1, source_target_pairs={{1,0},{2,1},{3,2},{4,3},{5,4},{6,5},{7,6},{9,8},{10,9},{11,10},{12... | collective-permute-start | bytes 9992 | tf_op jit(solution)/shard_map/ppermute | solution.py:20
  167.7 5.0 %collective-permute-start.8 = (f32[4,8,1,384]{3,2,1,0:T(1,128)S(1)}, f32[4,8,1,384]{3,2,1,0:T(1,128)S(1)}, u32[]{:S(2)}, u32[]{:S(2)}) collective-permute-start(f32[4,8,1,384]{3,2,1,0:T(1,128)S(1)} %get-tuple-element.62), channel_id=1, source_target_pairs={{0,8},{8,16},{16,24},{1,9},{9,17},{17,25},{2,10},{10,18},{18,26},{... | collective-permute-start | bytes 147464 | tf_op jit(solution)/shard_map/ppermute | solution.py:19
  170.8 3.4 %collective-permute-start.9 = (f32[4,8,1,384]{3,2,1,0:T(1,128)S(1)}, f32[4,8,1,384]{3,2,1,0:T(1,128)S(1)}, u32[]{:S(2)}, u32[]{:S(2)}) collective-permute-start(f32[4,8,1,384]{3,2,1,0:T(1,128)S(1)} %get-tuple-element.63), channel_id=1, source_target_pairs={{8,0},{16,8},{24,16},{9,1},{17,9},{25,17},{10,2},{18,10},{26,18},{... | collective-permute-start | bytes 147464 | tf_op jit(solution)/shard_map/ppermute | solution.py:20
  174.5 26.0 %collective-permute-start.10 = (f32[4,8,26,1]{3,2,1,0:T(8,128)S(1)}, f32[4,8,26,1]{3,2,1,0:T(8,128)S(1)}, u32[]{:S(2)}, u32[]{:S(2)}) collective-permute-start(f32[4,8,26,1]{3,2,1,0:T(8,128)S(1)} %get-tuple-element.46), channel_id=1, source_target_pairs={{0,1},{1,2},{2,3},{3,4},{4,5},{5,6},{6,7},{8,9},{9,10},{10,11},{11... | collective-permute-start | bytes 9992 | tf_op jit(solution)/shard_map/ppermute | solution.py:19
  178.9 21.6 %collective-permute-start.11 = (f32[4,8,26,1]{3,2,1,0:T(8,128)S(1)}, f32[4,8,26,1]{3,2,1,0:T(8,128)S(1)}, u32[]{:S(2)}, u32[]{:S(2)}) collective-permute-start(f32[4,8,26,1]{3,2,1,0:T(8,128)S(1)} %get-tuple-element.47), channel_id=1, source_target_pairs={{1,0},{2,1},{3,2},{4,3},{5,4},{6,5},{7,6},{9,8},{10,9},{11,10},{12... | collective-permute-start | bytes 9992 | tf_op jit(solution)/shard_map/ppermute | solution.py:20
  206.1 8.3 %copy-start.2 = (f32[1,8,24,384]{3,2,1,0:T(8,128)}, f32[1,8,24,384]{3,2,1,0:T(8,128)S(1)}, u32[]{:S(2)}) copy-start(f32[1,8,24,384]{3,2,1,0:T(8,128)S(1)} %get-tuple-element.11) | copy-start | bytes 884740
  289.8 11.1 %collective-permute-start.14 = (f32[4,8,26,1]{3,2,1,0:T(8,128)S(1)}, f32[4,8,26,1]{3,2,1,0:T(8,128)S(1)}, u32[]{:S(2)}, u32[]{:S(2)}) collective-permute-start(f32[4,8,26,1]{3,2,1,0:T(8,128)S(1)} %get-tuple-element.44), channel_id=1, source_target_pairs={{1,0},{2,1},{3,2},{4,3},{5,4},{6,5},{7,6},{9,8},{10,9},{11,10},{12... | collective-permute-start | bytes 9992 | tf_op jit(solution)/shard_map/ppermute | solution.py:20
  291.1 18.0 %collective-permute-start.15 = (f32[4,8,26,1]{3,2,1,0:T(8,128)S(1)}, f32[4,8,26,1]{3,2,1,0:T(8,128)S(1)}, u32[]{:S(2)}, u32[]{:S(2)}) collective-permute-start(f32[4,8,26,1]{3,2,1,0:T(8,128)S(1)} %get-tuple-element.45), channel_id=1, source_target_pairs={{0,1},{1,2},{2,3},{3,4},{4,5},{5,6},{6,7},{8,9},{9,10},{10,11},{11... | collective-permute-start | bytes 9992 | tf_op jit(solution)/shard_map/ppermute | solution.py:19
  310.4 0.9 copy-start.6
  310.4 1.1 copy-start.7
  310.4 1.1 copy-start.8
  310.4 1.1 copy-start.9
  311.5 1.0 copy-start.3
  311.5 1.0 copy-start.4
  312.5 1.1 copy-start.5
Sparse Core Ops, SparseCore 0:
  11.0 34.0 all-reduce.1
  289.5 15.4 all-gather.1
where the time goes:
time: 325 us; the launch traced here: 323 us
  blocking collectives  135 us (42%)
  waiting for transfers between devices  55.4 us (17%)
  local copies, waits for them, and re-layouts  40.7 us (13%)
  other arithmetic  36.6 us (11%)
  starting transfers between devices  34.8 us (11%)
  between operations  16.1 us (5%)
  matrix products  5.11 us (2%)
    all_gather x1, blocking collectives, on_device(): lax.all_gather(columns, 'gy', axis=3, tiled=True)  50.3 us
    ppermute x8, waiting for transfers between devices, extended(): before = lax.ppermute(last, axis, up)  48.7 us
    psum x1, blocking collectives, on_device(): row_pair = lax.psum(row_pair, 'gy')  39.1 us
    all_gather x1, blocking collectives, on_device(): lax.all_gather(coarse, 'gy', axis=3, tiled=True)  36 us
    ppermute x8, starting transfers between devices, extended(): before = lax.ppermute(last, axis, up)  24.2 us
    reshape x1, local copies, waits for them, and re-layouts, on_device(): fields[:3].reshape(3, levels, coarse_cols, 3, coarse_rows, 3)  21.9 us
    reduce_sum x1, other arithmetic, on_device(): fields[:3].reshape(3, levels, coarse_cols, 3, coarse_rows, 3)  14.8 us
    ppermute x8, starting transfers between devices, extended(): after = lax.ppermute(initial, axis, down)  10.5 us
  transfers between devices with their start and end apart: 18, of which 5 were waited for; matrix products, arithmetic and copies ran while one was open for 22% of the time, Pallas kernels for 0%

commit v1 on v0

--- a/solution.py
+++ b/solution.py
@@ -89,7 +89,11 @@
             take_slab(shift_y + span_y, index_y, parent_rows, 3),
         ]
     )
-    row_pair = lax.psum(row_pair, "gy")
+    peers, summed = (lax.axis_size("gy"), row_pair)
+    for reach in [1 << k for k in range(peers.bit_length() - 1)]:
+        swap = [(i_2, i_2 ^ reach) for i_2 in range(peers)]
+        summed = summed + lax.ppermute(summed, "gy", swap)
+    row_pair = summed
     column_first = shift_y + index_y * coarse_rows - 1
     row_first = shift_x + index_x * coarse_cols - 1
     column_strip = place_along(

time: 325 us -> 300 us (0.923)
  blocking collectives: 135 us -> 93.4 us
  starting transfers between devices: 34.8 us -> 44.6 us
  waiting for transfers between devices: 55.4 us -> 63 us
    psum x1 -> x0, blocking collectives: 39.1 us -> none  [on_device(): row_pair = lax.psum(row_pair, 'gy')]
    ppermute x8, waiting for transfers between devices: 48.7 us -> 36.2 us  [extended(): before = lax.ppermute(last, axis, up)]
    ppermute x8, waiting for transfers between devices: 6.69 us -> 15.7 us  [extended(): after = lax.ppermute(initial, axis, down)]
    ppermute x0 -> x3, waiting for transfers between devices: none -> 8.63 us  [on_device(): summed = summed + lax.ppermute(summed, 'gy', swap)]
    ppermute x0 -> x3, starting transfers between devices: none -> 7.33 us  [on_device(): summed = summed + lax.ppermute(summed, 'gy', swap)]
  transfers between devices with their start and end apart: 18 -> 21, of which waited for: 5 -> 9; matrix products, arithmetic and copies ran while one was open for 22% -> 23% of each run, Pallas kernels for 0% -> 0%
where the time goes in v1:
time: 300 us; the launch traced here: 298 us
  blocking collectives  93.4 us (31%)
  waiting for transfers between devices  63 us (21%)
  starting transfers between devices  44.6 us (15%)
  local copies, waits for them, and re-layouts  39.5 us (13%)
  other arithmetic  36.5 us (12%)
  between operations  16 us (5%)
  matrix products  5.1 us (2%)
    all_gather x1, blocking collectives, on_device(): lax.all_gather(columns, 'gy', axis=3, tiled=True)  50.5 us
    all_gather x1, blocking collectives, on_device(): lax.all_gather(coarse, 'gy', axis=3, tiled=True)  36.3 us
    ppermute x8, waiting for transfers between devices, extended(): before = lax.ppermute(last, axis, up)  36.2 us
    ppermute x8, starting transfers between devices, extended(): before = lax.ppermute(last, axis, up)  26.9 us
    reshape x1, local copies, waits for them, and re-layouts, on_device(): fields[:3].reshape(3, levels, coarse_cols, 3, coarse_rows, 3)  21.9 us
    ppermute x8, waiting for transfers between devices, extended(): after = lax.ppermute(initial, axis, down)  15.7 us
    reduce_sum x1, other arithmetic, on_device(): fields[:3].reshape(3, levels, coarse_cols, 3, coarse_rows, 3)  14.8 us
    ppermute x8, starting transfers between devices, extended(): after = lax.ppermute(initial, axis, down)  10.3 us
  transfers between devices with their start and end apart: 21, of which 9 were waited for; matrix products, arithmetic and copies ran while one was open for 23% of the time, Pallas kernels for 0%

profile of v1, /device:TPU:0, one launch (start us, length us, event | category | flops | bytes accessed | tf_op | source)
XLA Modules:
  0.0 298.1 jit_solution(8221006339014456606)
XLA Ops:
  7.9 1.5 constant_dynamic-slice_fusion.3
  10.0 3.0 %collective-permute-start = (f32[2,4,8,24]{2,1,0,3:T(4,128)S(1)}, f32[2,4,8,24]{2,1,0,3:T(4,128)S(1)}, u32[]{:S(2)}, u32[]{:S(2)}) collective-permute-start(f32[2,4,8,24]{2,1,0,3:T(4,128)S(1)} %copy.42), channel_id=1, source_target_pairs={{0,1},{1,0},{2,3},{3,2},{4,5},{5,4},{6,7},{7,6},{8,9},{9,8},{10,11... | collective-permute-start | bytes 18440 | tf_op jit(solution)/shard_map/ppermute | solution.py:95
  15.4 1.5 collective-permute-start.3
  18.2 1.6 collective-permute-start.1
  19.9 3.0 %collective-permute-done.1 = f32[2,4,8,24]{2,1,0,3:T(4,128)S(1)} collective-permute-done((f32[2,4,8,24]{2,1,0,3:T(4,128)S(1)}, f32[2,4,8,24]{2,1,0,3:T(4,128)S(1)}, u32[]{:S(2)}, u32[]{:S(2)}) %collective-permute-start.1) | collective-permute-done | bytes 6176 | tf_op jit(solution)/shard_map/ppermute | solution.py:95
  22.9 2.7 collective-permute-start.2
  25.6 5.6 %collective-permute-done.2 = f32[2,4,8,24]{2,1,0,3:T(4,128)S(1)} collective-permute-done((f32[2,4,8,24]{2,1,0,3:T(4,128)S(1)}, f32[2,4,8,24]{2,1,0,3:T(4,128)S(1)}, u32[]{:S(2)}, u32[]{:S(2)}) %collective-permute-start.2) | collective-permute-done | bytes 6176 | tf_op jit(solution)/shard_map/ppermute | solution.py:95
  31.2 6.6 %all_gather.12 = f32[2,4,8,96]{2,1,0,3:T(4,128)S(1)} all-gather(f32[2,4,8,24]{2,1,0,3:T(4,128)S(1)} %add.121), channel_id=1, replica_groups=mesh['gx'=4,'gy'=8] {'gx'}, dimensions={3}, use_global_device_ids=true | all-gather | bytes 30720 | tf_op jit(solution)/shard_map/all_gather | solution.py:103
  40.0 3.2 %collective-permute-start.5 = (f32[4,8,26,1]{3,2,1,0:T(8,128)}, f32[4,8,26,1]{3,2,1,0:T(8,128)}, u32[]{:S(2)}, u32[]{:S(2)}) collective-permute-start(f32[4,8,26,1]{3,2,1,0:T(8,128)} %get-tuple-element.50), channel_id=1, source_target_pairs={{0,1},{1,2},{2,3},{3,4},{4,5},{5,6},{6,7},{8,9},{9,10},{10,11},{11... | collective-permute-start | bytes 9992 | tf_op jit(solution)/shard_map/ppermute | solution.py:19
  44.5 2.5 all-reduce.2.cloned.1.call-done
  47.0 50.5 %all_gather.13 = f32[2,4,8,3072]{3,2,1,0:T(8,128)S(1)} all-gather(f32[2,4,8,384]{3,2,1,0:T(8,128)} %all-reduce.2.cloned.1.call-done), channel_id=1, replica_groups=mesh['gx'=4,'gy'=8] {'gy'}, dimensions={3}, use_global_device_ids=true | all-gather | bytes 884736 | tf_op jit(solution)/shard_map/all_gather | solution.py:100
  100.0 3.1 %fusion.2 = f32[4,8,26,386]{3,2,1,0:T(8,128)S(1)} fusion(f32[4,8,26,1]{3,2,1,0:T(8,128)} %collective-permute-done.6, f32[4,8,1,384]{3,2,1,0:T(1,128)S(1)} %collective-permute-done.4, f32[4,8,24,384]{3,2,1,0:T(8,128)S(1)} %copy-done.1, f32[4,8,1,384]{3,2,1,0:T(1,128)S(1)} %collective-permute-done.3, f32[4,8,26,1]{3,2,1,0:T(8,128)} %collective-permute-done.5, ...), kind=kLoop, calls=%fused_computation.3 | loop fusion | flops 2569216 | bytes 2675512 | tf_op jit(solution)/shard_map/jit(_where)/select_n | solution.py:122
  105.4 1.3 collective-permute-start.7
  109.3 5.1 %collective-permute-start.16 = (f32[4,8,1,384]{3,2,1,0:T(1,128)}, f32[4,8,1,384]{3,2,1,0:T(1,128)S(1)}, u32[]{:S(2)}, u32[]{:S(2)}) collective-permute-start(f32[4,8,1,384]{3,2,1,0:T(1,128)} %get-tuple-element.58), channel_id=1, source_target_pairs={{0,8},{8,16},{16,24},{1,9},{9,17},{17,25},{2,10},{10,18},{18,26},{... | collective-permute-start | bytes 147464 | tf_op jit(solution)/shard_map/ppermute | solution.py:19
  116.0 4.8 %collective-permute-start.9 = (f32[4,8,26,1]{3,2,1,0:T(8,128)S(1)}, f32[4,8,26,1]{3,2,1,0:T(8,128)S(1)}, u32[]{:S(2)}, u32[]{:S(2)}) collective-permute-start(f32[4,8,26,1]{3,2,1,0:T(8,128)S(1)} %get-tuple-element.48), channel_id=1, source_target_pairs={{0,1},{1,2},{2,3},{3,4},{4,5},{5,6},{6,7},{8,9},{9,10},{10,11},{11... | collective-permute-start | bytes 9992 | tf_op jit(solution)/shard_map/ppermute | solution.py:19
  121.6 9.0 %collective-permute-done.10 = f32[4,8,26,1]{3,2,1,0:T(8,128)S(1)} collective-permute-done((f32[4,8,26,1]{3,2,1,0:T(8,128)S(1)}, f32[4,8,26,1]{3,2,1,0:T(8,128)S(1)}, u32[]{:S(2)}, u32[]{:S(2)}) %collective-permute-start.10) | collective-permute-done | bytes 3360 | tf_op jit(solution)/shard_map/ppermute | solution.py:20
  130.6 7.7 %collective-permute-done.9 = f32[4,8,26,1]{3,2,1,0:T(8,128)S(1)} collective-permute-done((f32[4,8,26,1]{3,2,1,0:T(8,128)S(1)}, f32[4,8,26,1]{3,2,1,0:T(8,128)S(1)}, u32[]{:S(2)}, u32[]{:S(2)}) %collective-permute-start.9) | collective-permute-done | bytes 3360 | tf_op jit(solution)/shard_map/ppermute | solution.py:19
  138.3 2.6 fusion.5
  143.2 2.1 collective-permute-start.11
  147.3 1.5 collective-permute-done.12
  149.0 4.4 %collective-permute-start.13 = (f32[4,8,26,1]{3,2,1,0:T(8,128)S(1)}, f32[4,8,26,1]{3,2,1,0:T(8,128)S(1)}, u32[]{:S(2)}, u32[]{:S(2)}) collective-permute-start(f32[4,8,26,1]{3,2,1,0:T(8,128)S(1)} %get-tuple-element.46), channel_id=1, source_target_pairs={{0,1},{1,2},{2,3},{3,4},{4,5},{5,6},{6,7},{8,9},{9,10},{10,11},{11... | collective-permute-start | bytes 9992 | tf_op jit(solution)/shard_map/ppermute | solution.py:19
  154.8 20.3 %collective-permute-done.13 = f32[4,8,26,1]{3,2,1,0:T(8,128)S(1)} collective-permute-done((f32[4,8,26,1]{3,2,1,0:T(8,128)S(1)}, f32[4,8,26,1]{3,2,1,0:T(8,128)S(1)}, u32[]{:S(2)}, u32[]{:S(2)}) %collective-permute-start.13) | collective-permute-done | bytes 3360 | tf_op jit(solution)/shard_map/ppermute | solution.py:19
  175.1 2.6 fusion.8
  180.7 8.3 %copy.54 = f32[3,8,24,384]{1,3,2,0:T(8,128)} copy(f32[3,8,24,384]{3,2,1,0:T(8,128)S(1)} %pad_maximum_fusion.10) | data formatting | bytes 1769472 | tf_op jit(solution)/shard_map/stack | solution.py:41
  188.9 21.9 %reshape.170 = f32[3,8,8,3,128,3]{1,5,4,3,2,0:T(4,128)} reshape(f32[3,8,24,384]{1,3,2,0:T(8,128)} %copy.54) | data formatting | bytes 1769472 | tf_op jit(solution)/shard_map/reshape | solution.py:124
  210.8 14.8 %reduce_sum.9 = f32[3,8,8,128]{1,3,2,0:T(8,128)S(1)} reduce(f32[3,8,8,3,128,3]{1,5,4,3,2,0:T(4,128)} %reshape.170, f32[]{:T(128)} %constant.17.clone.1), dimensions={3,5}, to_apply=%region_1.2 | reduce | flops 196608 | bytes 983044 | tf_op jit(solution)/shard_map/reduce_sum | solution.py:124
  226.1 36.3 %all_gather.14 = f32[3,8,8,1024]{3,2,1,0:T(8,128)S(1)} all-gather(f32[3,8,8,128]{3,2,1,0:T(8,128)S(1)} %broadcast_multiply_fusion), channel_id=1, replica_groups=mesh['gx'=4,'gy'=8] {'gy'}, dimensions={3}, use_global_device_ids=true | all-gather | bytes 884736 | tf_op jit(solution)/shard_map/all_gather | solution.py:128
  262.4 1.7 fusion.13
  265.9 4.6 %collective-permute-start.18 = (f32[4,8,26,1]{3,2,1,0:T(8,128)S(1)}, f32[4,8,26,1]{3,2,1,0:T(8,128)S(1)}, u32[]{:S(2)}, u32[]{:S(2)}) collective-permute-start(f32[4,8,26,1]{3,2,1,0:T(8,128)S(1)} %get-tuple-element.45), channel_id=1, source_target_pairs={{0,1},{1,2},{2,3},{3,4},{4,5},{5,6},{6,7},{8,9},{9,10},{10,11},{11... | collective-permute-start | bytes 9992 | tf_op jit(solution)/shard_map/ppermute | solution.py:19
  270.5 5.2 %collective-permute-done.17 = f32[4,8,26,1]{3,2,1,0:T(8,128)S(1)} collective-permute-done((f32[4,8,26,1]{3,2,1,0:T(8,128)S(1)}, f32[4,8,26,1]{3,2,1,0:T(8,128)S(1)}, u32[]{:S(2)}, u32[]{:S(2)}) %collective-permute-start.17) | collective-permute-done | bytes 3360 | tf_op jit(solution)/shard_map/ppermute | solution.py:20
  275.7 8.2 %collective-permute-done.18 = f32[4,8,26,1]{3,2,1,0:T(8,128)S(1)} collective-permute-done((f32[4,8,26,1]{3,2,1,0:T(8,128)S(1)}, f32[4,8,26,1]{3,2,1,0:T(8,128)S(1)}, u32[]{:S(2)}, u32[]{:S(2)}) %collective-permute-start.18) | collective-permute-done | bytes 3360 | tf_op jit(solution)/shard_map/ppermute | solution.py:19
  288.4 1.8 fusion.15
  (120 shorter events, 33.4 us)
Async XLA Ops:
  7.2 39.8 %all-reduce.2.cloned.1.call-start = ((), (), s32[]{:S(2)}) async-start(), calls=%async_computation | async-start | bytes 196608 | tf_op jit(solution)/shard_map/psum | solution.py:85
  7.9 5.9 %copy-start = (f32[4,8,24,384]{3,2,1,0:T(8,128)S(1)}, f32[4,8,24,384]{3,2,1,0:T(8,128)}, u32[]{:S(2)}) copy-start(f32[4,8,24,384]{3,2,1,0:T(8,128)} %param.5) | copy-start | bytes 3538948
  9.4 5.9 %copy-start.1 = (f32[4,8,24,384]{3,2,1,0:T(8,128)S(1)}, f32[4,8,24,384]{3,2,1,0:T(8,128)}, u32[]{:S(2)}) copy-start(f32[4,8,24,384]{3,2,1,0:T(8,128)} %param.4) | copy-start | bytes 3538948
  10.0 8.1 %collective-permute-start = (f32[2,4,8,24]{2,1,0,3:T(4,128)S(1)}, f32[2,4,8,24]{2,1,0,3:T(4,128)S(1)}, u32[]{:S(2)}, u32[]{:S(2)}) collective-permute-start(f32[2,4,8,24]{2,1,0,3:T(4,128)S(1)} %copy.42), channel_id=1, source_target_pairs={{0,1},{1,0},{2,3},{3,2},{4,5},{5,4},{6,7},{7,6},{8,9},{9,8},{10,11... | collective-permute-start | bytes 18440 | tf_op jit(solution)/shard_map/ppermute | solution.py:95
  15.2 273.1 %all-gather.2.cloned.1.call-start = ((), (), s32[]{:S(2)}) async-start(), calls=%async_computation.1 | async-start | bytes 1474560 | tf_op jit(solution)/shard_map/all_gather | solution.py:131
  15.4 23.4 %collective-permute-start.3 = (f32[4,8,1,384]{3,2,1,0:T(1,128)S(1)}, f32[4,8,1,384]{3,2,1,0:T(1,128)S(1)}, u32[]{:S(2)}, u32[]{:S(2)}) collective-permute-start(f32[4,8,1,384]{3,2,1,0:T(1,128)S(1)} %get-tuple-element.68), channel_id=1, source_target_pairs={{0,8},{8,16},{16,24},{1,9},{9,17},{17,25},{2,10},{10,18},{18,26},{... | collective-permute-start | bytes 147464 | tf_op jit(solution)/shard_map/ppermute | solution.py:19
  16.8 21.9 %collective-permute-start.4 = (f32[4,8,1,384]{3,2,1,0:T(1,128)S(1)}, f32[4,8,1,384]{3,2,1,0:T(1,128)S(1)}, u32[]{:S(2)}, u32[]{:S(2)}) collective-permute-start(f32[4,8,1,384]{3,2,1,0:T(1,128)S(1)} %get-tuple-element.69), channel_id=1, source_target_pairs={{8,0},{16,8},{24,16},{9,1},{17,9},{25,17},{10,2},{18,10},{26,18},{... | collective-permute-start | bytes 147464 | tf_op jit(solution)/shard_map/ppermute | solution.py:20
  18.2 4.7 %collective-permute-start.1 = (f32[2,4,8,24]{2,1,0,3:T(4,128)S(1)}, f32[2,4,8,24]{2,1,0,3:T(4,128)S(1)}, u32[]{:S(2)}, u32[]{:S(2)}) collective-permute-start(f32[2,4,8,24]{2,1,0,3:T(4,128)S(1)} %add.119), channel_id=1, source_target_pairs={{0,2},{1,3},{2,0},{3,1},{4,6},{5,7},{6,4},{7,5},{8,10},{9,11},{10,... | collective-permute-start | bytes 18440 | tf_op jit(solution)/shard_map/ppermute | solution.py:95
  22.9 8.3 %collective-permute-start.2 = (f32[2,4,8,24]{2,1,0,3:T(4,128)S(1)}, f32[2,4,8,24]{2,1,0,3:T(4,128)S(1)}, u32[]{:S(2)}, u32[]{:S(2)}) collective-permute-start(f32[2,4,8,24]{2,1,0,3:T(4,128)S(1)} %add.120), channel_id=1, source_target_pairs={{0,4},{1,5},{2,6},{3,7},{4,0},{5,1},{6,2},{7,3},{8,12},{9,13},{10,... | collective-permute-start | bytes 18440 | tf_op jit(solution)/shard_map/ppermute | solution.py:95
  40.0 60.0 %collective-permute-start.5 = (f32[4,8,26,1]{3,2,1,0:T(8,128)}, f32[4,8,26,1]{3,2,1,0:T(8,128)}, u32[]{:S(2)}, u32[]{:S(2)}) collective-permute-start(f32[4,8,26,1]{3,2,1,0:T(8,128)} %get-tuple-element.50), channel_id=1, source_target_pairs={{0,1},{1,2},{2,3},{3,4},{4,5},{5,6},{6,7},{8,9},{9,10},{10,11},{11... | collective-permute-start | bytes 9992 | tf_op jit(solution)/shard_map/ppermute | solution.py:19
  43.2 56.7 %collective-permute-start.6 = (f32[4,8,26,1]{3,2,1,0:T(8,128)}, f32[4,8,26,1]{3,2,1,0:T(8,128)}, u32[]{:S(2)}, u32[]{:S(2)}) collective-permute-start(f32[4,8,26,1]{3,2,1,0:T(8,128)} %get-tuple-element.51), channel_id=1, source_target_pairs={{1,0},{2,1},{3,2},{4,3},{5,4},{6,5},{7,6},{9,8},{10,9},{11,10},{12... | collective-permute-start | bytes 9992 | tf_op jit(solution)/shard_map/ppermute | solution.py:20
  105.4 9.0 %collective-permute-start.7 = (f32[4,8,1,384]{3,2,1,0:T(1,128)S(1)}, f32[4,8,1,384]{3,2,1,0:T(1,128)S(1)}, u32[]{:S(2)}, u32[]{:S(2)}) collective-permute-start(f32[4,8,1,384]{3,2,1,0:T(1,128)S(1)} %get-tuple-element.64), channel_id=1, source_target_pairs={{0,8},{8,16},{16,24},{1,9},{9,17},{17,25},{2,10},{10,18},{18,26},{... | collective-permute-start | bytes 147464 | tf_op jit(solution)/shard_map/ppermute | solution.py:19
  106.7 7.7 %collective-permute-start.8 = (f32[4,8,1,384]{3,2,1,0:T(1,128)S(1)}, f32[4,8,1,384]{3,2,1,0:T(1,128)S(1)}, u32[]{:S(2)}, u32[]{:S(2)}) collective-permute-start(f32[4,8,1,384]{3,2,1,0:T(1,128)S(1)} %get-tuple-element.65), channel_id=1, source_target_pairs={{8,0},{16,8},{24,16},{9,1},{17,9},{25,17},{10,2},{18,10},{26,18},{... | collective-permute-start | bytes 147464 | tf_op jit(solution)/shard_map/ppermute | solution.py:20
  108.0 156.3 %collective-permute-start.15 = (f32[4,8,1,384]{3,2,1,0:T(1,128)}, f32[4,8,1,384]{3,2,1,0:T(1,128)S(1)}, u32[]{:S(2)}, u32[]{:S(2)}) collective-permute-start(f32[4,8,1,384]{3,2,1,0:T(1,128)} %get-tuple-element.59), channel_id=1, source_target_pairs={{8,0},{16,8},{24,16},{9,1},{17,9},{25,17},{10,2},{18,10},{26,18},{... | collective-permute-start | bytes 147464 | tf_op jit(solution)/shard_map/ppermute | solution.py:20
  109.3 155.0 %collective-permute-start.16 = (f32[4,8,1,384]{3,2,1,0:T(1,128)}, f32[4,8,1,384]{3,2,1,0:T(1,128)S(1)}, u32[]{:S(2)}, u32[]{:S(2)}) collective-permute-start(f32[4,8,1,384]{3,2,1,0:T(1,128)} %get-tuple-element.58), channel_id=1, source_target_pairs={{0,8},{8,16},{16,24},{1,9},{9,17},{17,25},{2,10},{10,18},{18,26},{... | collective-permute-start | bytes 147464 | tf_op jit(solution)/shard_map/ppermute | solution.py:19
  114.7 16.0 %collective-permute-start.10 = (f32[4,8,26,1]{3,2,1,0:T(8,128)S(1)}, f32[4,8,26,1]{3,2,1,0:T(8,128)S(1)}, u32[]{:S(2)}, u32[]{:S(2)}) collective-permute-start(f32[4,8,26,1]{3,2,1,0:T(8,128)S(1)} %get-tuple-element.49), channel_id=1, source_target_pairs={{1,0},{2,1},{3,2},{4,3},{5,4},{6,5},{7,6},{9,8},{10,9},{11,10},{12... | collective-permute-start | bytes 9992 | tf_op jit(solution)/shard_map/ppermute | solution.py:20
  116.0 22.3 %collective-permute-start.9 = (f32[4,8,26,1]{3,2,1,0:T(8,128)S(1)}, f32[4,8,26,1]{3,2,1,0:T(8,128)S(1)}, u32[]{:S(2)}, u32[]{:S(2)}) collective-permute-start(f32[4,8,26,1]{3,2,1,0:T(8,128)S(1)} %get-tuple-element.48), channel_id=1, source_target_pairs={{0,1},{1,2},{2,3},{3,4},{4,5},{5,6},{6,7},{8,9},{9,10},{10,11},{11... | collective-permute-start | bytes 9992 | tf_op jit(solution)/shard_map/ppermute | solution.py:19
  143.2 4.0 %collective-permute-start.11 = (f32[4,8,1,384]{3,2,1,0:T(1,128)S(1)}, f32[4,8,1,384]{3,2,1,0:T(1,128)S(1)}, u32[]{:S(2)}, u32[]{:S(2)}) collective-permute-start(f32[4,8,1,384]{3,2,1,0:T(1,128)S(1)} %get-tuple-element.62), channel_id=1, source_target_pairs={{0,8},{8,16},{16,24},{1,9},{9,17},{17,25},{2,10},{10,18},{18,26},{... | collective-permute-start | bytes 147464 | tf_op jit(solution)/shard_map/ppermute | solution.py:19
  145.3 3.4 %collective-permute-start.12 = (f32[4,8,1,384]{3,2,1,0:T(1,128)S(1)}, f32[4,8,1,384]{3,2,1,0:T(1,128)S(1)}, u32[]{:S(2)}, u32[]{:S(2)}) collective-permute-start(f32[4,8,1,384]{3,2,1,0:T(1,128)S(1)} %get-tuple-element.63), channel_id=1, source_target_pairs={{8,0},{16,8},{24,16},{9,1},{17,9},{25,17},{10,2},{18,10},{26,18},{... | collective-permute-start | bytes 147464 | tf_op jit(solution)/shard_map/ppermute | solution.py:20
  149.0 26.0 %collective-permute-start.13 = (f32[4,8,26,1]{3,2,1,0:T(8,128)S(1)}, f32[4,8,26,1]{3,2,1,0:T(8,128)S(1)}, u32[]{:S(2)}, u32[]{:S(2)}) collective-permute-start(f32[4,8,26,1]{3,2,1,0:T(8,128)S(1)} %get-tuple-element.46), channel_id=1, source_target_pairs={{0,1},{1,2},{2,3},{3,4},{4,5},{5,6},{6,7},{8,9},{9,10},{10,11},{11... | collective-permute-start | bytes 9992 | tf_op jit(solution)/shard_map/ppermute | solution.py:19
  153.5 21.6 %collective-permute-start.14 = (f32[4,8,26,1]{3,2,1,0:T(8,128)S(1)}, f32[4,8,26,1]{3,2,1,0:T(8,128)S(1)}, u32[]{:S(2)}, u32[]{:S(2)}) collective-permute-start(f32[4,8,26,1]{3,2,1,0:T(8,128)S(1)} %get-tuple-element.47), channel_id=1, source_target_pairs={{1,0},{2,1},{3,2},{4,3},{5,4},{6,5},{7,6},{9,8},{10,9},{11,10},{12... | collective-permute-start | bytes 9992 | tf_op jit(solution)/shard_map/ppermute | solution.py:20
  180.6 8.4 %copy-start.2 = (f32[1,8,24,384]{3,2,1,0:T(8,128)}, f32[1,8,24,384]{3,2,1,0:T(8,128)S(1)}, u32[]{:S(2)}) copy-start(f32[1,8,24,384]{3,2,1,0:T(8,128)S(1)} %get-tuple-element.11) | copy-start | bytes 884740
  264.6 11.1 %collective-permute-start.17 = (f32[4,8,26,1]{3,2,1,0:T(8,128)S(1)}, f32[4,8,26,1]{3,2,1,0:T(8,128)S(1)}, u32[]{:S(2)}, u32[]{:S(2)}) collective-permute-start(f32[4,8,26,1]{3,2,1,0:T(8,128)S(1)} %get-tuple-element.44), channel_id=1, source_target_pairs={{1,0},{2,1},{3,2},{4,3},{5,4},{6,5},{7,6},{9,8},{10,9},{11,10},{12... | collective-permute-start | bytes 9992 | tf_op jit(solution)/shard_map/ppermute | solution.py:20
  265.9 18.0 %collective-permute-start.18 = (f32[4,8,26,1]{3,2,1,0:T(8,128)S(1)}, f32[4,8,26,1]{3,2,1,0:T(8,128)S(1)}, u32[]{:S(2)}, u32[]{:S(2)}) collective-permute-start(f32[4,8,26,1]{3,2,1,0:T(8,128)S(1)} %get-tuple-element.45), channel_id=1, source_target_pairs={{0,1},{1,2},{2,3},{3,4},{4,5},{5,6},{6,7},{8,9},{9,10},{10,11},{11... | collective-permute-start | bytes 9992 | tf_op jit(solution)/shard_map/ppermute | solution.py:19
  285.1 0.9 copy-start.6
  285.1 1.1 copy-start.7
  285.1 1.1 copy-start.8
  285.2 1.1 copy-start.9
  286.2 1.0 copy-start.3
  286.2 1.0 copy-start.4
  287.3 1.1 copy-start.5
Sparse Core Ops, SparseCore 0:
  15.3 31.5 all-reduce.1
  264.3 15.4 all-gather.1
